TPU v7x, 256 devices: a whole 4x4x8 slice. The times are simulated.
256 devices in a mesh: row: 8 (over y, core), leaf: 32 (over x, z).
Axes of the slice: x: 4, y: 4, z: 8, core: 2. Of those that a mesh axis runs over, the one named last changes fastest.
Arguments:
- diag_blocks: float32 [32, 24, 256, 256], P('leaf', 'row'), as said below
- panel: float32 [32, 24, 768, 256], P('leaf', None, 'row'), may hold values from -1.5 to 1.5
- parent: int32 [32, 24, 1], replicated, may hold values from 0 to 31; in each aligned block of 24 rows (0 to 23, 24 to 47, ..., all dimensions but the last counted through in order) at most 2 rows name the same one
- rel: int32 [32, 24, 6], replicated, may hold values from 0 to 7, as said below
- front: float32 [32, 1024, 1024], P('leaf', None, 'row'), may hold values from -6 to 6
Outputs:
- factor_diag: float32 [32, 24, 256, 256], P('leaf', 'row')
- factor_panel: bfloat16 [32, 24, 768, 256], P('leaf', None, 'row')
- new_front: float32 [32, 1024, 1024], P('leaf', None, 'row')
Inputs may be any that keep to these rules, and one draw needn't show every extreme that they name: Among the 24 supernodes of one leaf index at most 2 have the same parent owner, and some leaf index reaches 2. `rel`: the 6 entries of each supernode name different blocks of the parent's front, in rising order. `diag_blocks`: every block is symmetric positive definite.
All inputs are finite; a program needn't handle non-finite values.
Results may differ from a plain program's by a relative error of at most 0.0011.
Values may be sent and summed in bfloat16 or wider, within the bound.
No kernel may reach another device: no remote copies, remote signals or barrier semaphores. Data moves between devices by JAX's collectives and lax.ppermute only.
A program may use at most 128 MiB of HBM per device.

v0:
```python
import jax
import jax.numpy as jnp
from jax import lax
from jax.sharding import PartitionSpec as P

W = 256
BS = 128
FB = 8
P_SIZE = 6


def on_device(diag_blocks, panel, parent, rel, front):
    row_count = lax.axis_size("row")
    leaf_count = lax.axis_size("leaf")
    row_index = lax.axis_index("row")
    leaf_index = lax.axis_index("leaf")
    own_factor = jnp.linalg.cholesky(diag_blocks[0])
    factors_all = lax.all_gather(own_factor, "row", axis=0, tiled=True)
    solved = jax.scipy.linalg.solve_triangular(
        factors_all, jnp.swapaxes(panel[0], 1, 2), lower=True
    )
    panel_rows = jnp.swapaxes(solved, 1, 2).astype(jnp.bfloat16)
    owners = parent[:, :, 0]
    supernodes = owners.shape[1]
    most_slots = max(2, 3 * supernodes // (2 * leaf_count))
    node_ids = jnp.arange(supernodes, dtype=jnp.int32)
    before = node_ids[None, :] < node_ids[:, None]
    same_owner = owners[:, :, None] == owners[:, None, :]
    position = jnp.sum(jnp.logical_and(same_owner, before[None]), axis=2)
    slot_ids = jnp.arange(most_slots, dtype=jnp.int32)
    targets = jnp.arange(leaf_count, dtype=jnp.int32)
    my_owner = lax.dynamic_index_in_dim(owners, leaf_index, 0, keepdims=False)
    my_position = lax.dynamic_index_in_dim(position, leaf_index, 0, keepdims=False)
    send_match = jnp.logical_and(
        my_owner[None, None, :] == targets[:, None, None],
        my_position[None, None, :] == slot_ids[None, :, None],
    )
    send_child = jnp.sum(jnp.where(send_match, node_ids, 0), axis=2)
    send_valid = jnp.any(send_match, axis=2)
    recv_match = jnp.logical_and(
        owners[:, None, :] == leaf_index, position[:, None, :] == slot_ids[None, :, None]
    )
    recv_valid = jnp.any(recv_match, axis=2)
    recv_blocks = jnp.sum(jnp.where(recv_match[..., None], rel[:, None, :, :], 0), axis=2)
    blocks_per_row = FB // row_count
    owned_blocks = row_index * blocks_per_row + jnp.arange(blocks_per_row, dtype=jnp.int32)
    columns = blocks_per_row * BS
    full_panel = lax.all_gather(panel_rows, "row", axis=1, tiled=True)
    my_blocks = lax.dynamic_index_in_dim(rel, leaf_index, 0, keepdims=False)
    leading = full_panel.shape[:-2]
    selector = (my_blocks[..., None, :] == owned_blocks[:, None]).astype(jnp.bfloat16)
    parted = full_panel.reshape(leading + (P_SIZE, BS, W))
    picked = jnp.einsum(
        "...tp,...pbw->...tbw", selector, parted, preferred_element_type=jnp.float32
    ).astype(jnp.bfloat16)
    picked = picked.reshape(leading + (columns, W))
    child_updates = jnp.einsum(
        "...iw,...cw->...ic", full_panel, picked, preferred_element_type=jnp.float32
    ).astype(jnp.bfloat16)
    outgoing = jnp.where(
        send_valid[..., None, None],
        jnp.take(child_updates, send_child, axis=0),
        jnp.zeros((), jnp.bfloat16),
    )
    incoming = lax.all_to_all(outgoing, "leaf", split_axis=0, concat_axis=0, tiled=True)
    front_ids = jnp.arange(FB, dtype=jnp.int32)
    placing = jnp.logical_and(
        recv_blocks[..., None, :] == front_ids[:, None], recv_valid[..., None, None]
    ).astype(jnp.bfloat16)
    parted_updates = incoming.reshape(incoming.shape[0], incoming.shape[1], P_SIZE, BS, columns)
    assembled = jnp.einsum(
        "smfp,smpic->fic", placing, parted_updates, preferred_element_type=jnp.float32
    )
    new_front = front[0] - assembled.reshape(FB * BS, columns)
    return (own_factor[None], panel_rows[None], new_front[None])


def solution(mesh):
    in_specs = (
        P("leaf", "row", None, None),
        P("leaf", None, "row", None),
        P(),
        P(),
        P("leaf", None, "row"),
    )
    out_specs = (P("leaf", "row", None, None), P("leaf", None, "row", None), P("leaf", None, "row"))
    return jax.shard_map(
        on_device, mesh=mesh, in_specs=in_specs, out_specs=out_specs, check_vma=False
    )
```

profile of v0, /device:TPU:163, one launch (start us, length us, event | category | flops | bytes accessed | tf_op | source)
XLA Modules:
  0.0 1087.2 jit_solution(9359395064277232795)
XLA Ops:
  7.3 1.4 copy.66
  8.7 1.2 fusion.16
  10.0 35.2 %custom-call.17 = f32[3,128,128]{2,1,0:T(8,128)S(1)} custom-call(f32[3,128,128]{2,1,0:T(8,128)S(1)} %cholesky.122), custom_call_target="Cholesky" | custom-call | tf_op jit(solution)/shard_map/jit(cholesky)/cholesky | solution.py:17
  45.2 29.5 %custom-call.18 = f32[3,1,128,128]{2,3,1,0:T(8,128)S(1)} custom-call(f32[3,1,128,128]{3,2,1,0:T(8,128)S(1)} %select_bitcast_fusion), custom_call_target="InvertDiagBlocksLowerTriangular" | custom-call | tf_op jit(solution)/shard_map/jit(cholesky)/cholesky | solution.py:17
  75.6 35.2 %custom-call.19 = f32[3,128,128]{2,1,0:T(8,128)S(1)} custom-call(f32[3,128,128]{2,1,0:T(8,128)S(1)} %convolution_subtract_fusion), custom_call_target="Cholesky" | custom-call | tf_op jit(solution)/shard_map/jit(cholesky)/cholesky | solution.py:17
  111.0 1.0 select_select_fusion.1
  112.1 45.1 %all-gather.3.cloned.1.call-done = f32[24,256,256]{2,1,0:T(8,128)} async-done(((f32[3,256,256]{2,1,0:T(8,128)}), f32[24,256,256]{2,1,0:T(8,128)}) %all-gather.3.cloned.1.call-update) | async-done | bytes 6291472 | tf_op jit(solution)/shard_map/all_gather | solution.py:18
  157.3 6.3 broadcast_select_fusion
  163.7 10.5 while.1
  164.3 5.0 bitcast_dynamic-update-slice_fusion.2
  169.8 4.4 bitcast_dynamic-update-slice_fusion.2
  174.2 473.0 %custom-call.20 = f32[24,2,128,128]{2,3,1,0:T(8,128)} custom-call(f32[24,2,128,128]{3,2,1,0:T(8,128)} %bitcast.90), custom_call_target="InvertDiagBlocksLowerTriangular" | custom-call | tf_op jit(solution)/shard_map/jit(_solve_triangular)/vmap()/triangular_solve | solution.py:19
  647.2 2.9 fusion.32
  650.1 4.9 fusion.8
  655.1 1.5 fusion.11
  656.7 1.7 fusion.18
  660.5 54.8 %all-gather.5.cloned.1.call-done = bf16[24,768,256]{2,1,0:T(8,128)(2,1)} async-done(((bf16[24,96,256]{2,1,0:T(8,128)(2,1)}), bf16[24,768,256]{2,1,0:T(8,128)(2,1)}) %all-gather.5.cloned.1.call-update) | async-done | bytes 9437200 | tf_op jit(solution)/shard_map/all_gather | solution.py:48
  715.3 11.9 %fusion = bf16[24,1,128,256]{3,1,2,0:T(2,128)(2,1)} fusion(pred[24,6,1,1]{1,2,3,0:T(4,128)(4,1)S(1)} %copy.82, bf16[24,6,128,256]{3,2,1,0:T(8,128)(2,1)} %bitcast.84), kind=kOutput, calls=%fused_computation.3 | convolution fusion | flops 9437184 | bytes 11010192 | tf_op jit(solution)/shard_map/...tp,...pbw->...tbw/dot_general | solution.py:53
  727.2 6.1 convolution_convert_fusion
  733.3 9.5 gather_fusion
  742.8 11.0 %select_select_fusion = bf16[32,2,768,128]{3,2,1,0:T(8,128)(2,1)} fusion(bf16[32,2,768,128]{3,2,1,0:T(8,128)(2,1)} %bitcast.83, pred[32,2]{1,0:T(8,128)(4,1)S(1)} %copy.74, pred[32,2]{1,0:T(8,128)(4,1)S(1)} %copy.73), kind=kLoop, calls=%fused_computation.7 | loop fusion | flops 12582912 | bytes 25165952 | tf_op jit(solution)/shard_map/jit(_where)/select_n | solution.py:60
  753.9 9.2 all-to-all-start
  764.2 302.4 %all-to-all-done = bf16[32,2,768,128]{3,2,1,0:T(8,128)(2,1)} async-done(((bf16[32,2,768,128]{3,2,1,0:T(8,128)(2,1)}), bf16[32,2,768,128]{3,2,1,0:T(8,128)(2,1)}, u32[]{:S(2)}, u32[]{:S(2)}) %all-to-all-start) | async-done | bytes 12582944 | tf_op jit(solution)/shard_map/all_to_all | solution.py:65
  1066.6 12.8 %fusion.12 = f32[8,128,128]{2,0,1:T(8,128)S(1)} fusion(bf16[32,2,6,128,128]{4,3,2,1,0:T(8,128)(2,1)} %bitcast.24, s32[32,2,6]{0,2,1:T(8,128)S(1)} %select_reduce_fusion.2, pred[32,2]{0,1:T(4,128)(4,1)S(1)} %get-tuple-element.21), kind=kOutput, calls=%fused_computation.19 | convolution fusion | flops 100669440 | bytes 13108800 | tf_op jit(solution)/shard_map/smfp,smpic->fic/dot_general | solution.py:71
  (59 shorter events, 6.7 us)
Async XLA Ops:
  7.2 150.1 %all-gather.3.cloned.1.call-start = ((), (), s32[]{:S(2)}) async-start(), calls=%async_computation.1 | async-start | bytes 7077888 | tf_op jit(solution)/shard_map/all_gather | solution.py:18
  112.1 603.2 %all-gather.5.cloned.1.call-start = ((), (), s32[]{:S(2)}) async-start(), calls=%async_computation.2 | async-start | bytes 10616832 | tf_op jit(solution)/shard_map/all_gather | solution.py:48
  163.7 483.5 %copy-start.2 = (f32[1,24,96,256]{3,2,1,0:T(8,128)S(1)}, f32[1,24,96,256]{3,2,1,0:T(8,128)}, u32[]{:S(2)}) copy-start(f32[1,24,96,256]{3,2,1,0:T(8,128)} %param.6) | copy-start | bytes 7077892
  650.1 5.0 copy-start.1
  656.6 1.8 copy-start.5
  656.7 3.4 copy-start.4
  715.3 11.9 %copy-start = (bf16[24,768,256]{2,1,0:T(8,128)(2,1)S(1)}, bf16[24,768,256]{2,1,0:T(8,128)(2,1)}, u32[]{:S(2)}) copy-start(bf16[24,768,256]{2,1,0:T(8,128)(2,1)} %all-gather.5.cloned.1.call-done) | copy-start | bytes 28311556
  753.9 312.7 %all-to-all-start = ((bf16[32,2,768,128]{3,2,1,0:T(8,128)(2,1)}), bf16[32,2,768,128]{3,2,1,0:T(8,128)(2,1)}, u32[]{:S(2)}, u32[]{:S(2)}) async-start(bf16[32,2,768,128]{3,2,1,0:T(8,128)(2,1)} %select_select_fusion), calls=%async_computation | async-start | bytes 25165824 | tf_op jit(solution)/shard_map/all_to_all | solution.py:65
  1066.6 12.9 %copy-start.3 = (f32[1,1024,128]{2,1,0:T(8,128)S(1)}, f32[1,1024,128]{2,1,0:T(8,128)}, u32[]{:S(2)}) copy-start(f32[1,1024,128]{2,1,0:T(8,128)} %param.9) | copy-start | bytes 1572868
Sparse Core Ops, SparseCore 0:
  112.2 45.0 all-gather.2
  658.5 56.7 all-gather.4
where the time goes:
time: 1090 us
  other arithmetic  597 us (55%)
  waiting for transfers between devices  402 us (37%)
  matrix products  41.1 us (4%)
  local copies, waits for them, and re-layouts  23.2 us (2%)
  between operations  14.3 us (1%)
    another operation x3, other arithmetic, on_device(): jax.scipy.linalg.solve_triangular(factors_all, jnp.swapaxes(panel[0], 1,...  479 us
    all_to_all x1, waiting for transfers between devices, on_device(): lax.all_to_all(outgoing, 'leaf', split_axis=0, concat_axis=0, tiled=True)  302 us
    another operation x9, other arithmetic, on_device(): own_factor = jnp.linalg.cholesky(diag_blocks[0])  100 us
    all_gather x1, waiting for transfers between devices, on_device(): full_panel = lax.all_gather(panel_rows, 'row', axis=1, tiled=True)  54.8 us
    all_gather x1, waiting for transfers between devices, on_device(): factors_all = lax.all_gather(own_factor, 'row', axis=0, tiled=True)  45.1 us
  transfers between devices with their start and end apart: 3, of which 3 were waited for; matrix products, arithmetic and copies ran while one was open for 0% of the time, Pallas kernels for 0%

commit v1 on v0

--- a/solution.py
+++ b/solution.py
@@ -45,7 +45,9 @@
     blocks_per_row = FB // row_count
     owned_blocks = row_index * blocks_per_row + jnp.arange(blocks_per_row, dtype=jnp.int32)
     columns = blocks_per_row * BS
-    full_panel = lax.all_gather(panel_rows, "row", axis=1, tiled=True)
+    full_panel = jnp.concatenate(
+        lax.all_to_all(jnp.stack([panel_rows] * lax.axis_size("row")), "row", 0, 0), axis=1
+    )
     my_blocks = lax.dynamic_index_in_dim(rel, leaf_index, 0, keepdims=False)
     leading = full_panel.shape[:-2]
     selector = (my_blocks[..., None, :] == owned_blocks[:, None]).astype(jnp.bfloat16)

time: 1090 us -> 1150 us (1.055)
  waiting for transfers between devices: 402 us -> 442 us
  local copies, waits for them, and re-layouts: 23.2 us -> 36.6 us
    all_to_all x0 -> x1, waiting for transfers between devices: none -> 103 us  [on_device(): lax.all_to_all(jnp.stack([panel_rows] * lax.axis_size('row')), 'row', 0, 0)]
    all_gather x1 -> x0, waiting for transfers between devices: 54.8 us -> none  [on_device(): full_panel = lax.all_gather(panel_rows, 'row', axis=1, tiled=True)]
where the time goes in v1:
time: 1150 us
  other arithmetic  597 us (52%)
  waiting for transfers between devices  442 us (38%)
  matrix products  41 us (4%)
  local copies, waits for them, and re-layouts  36.6 us (3%)
  starting transfers between devices  14.6 us (1%)
  between operations  14.3 us (1%)
    another operation x3, other arithmetic, on_device(): jax.scipy.linalg.solve_triangular(factors_all, jnp.swapaxes(panel[0], 1,...  479 us
    all_to_all x1, waiting for transfers between devices, on_device(): lax.all_to_all(outgoing, 'leaf', split_axis=0, concat_axis=0, tiled=True)  294 us
    all_to_all x1, waiting for transfers between devices, on_device(): lax.all_to_all(jnp.stack([panel_rows] * lax.axis_size('row')), 'row', 0, 0)  103 us
    another operation x9, other arithmetic, on_device(): own_factor = jnp.linalg.cholesky(diag_blocks[0])  100 us
    all_gather x1, waiting for transfers between devices, on_device(): factors_all = lax.all_gather(own_factor, 'row', axis=0, tiled=True)  45.2 us
  transfers between devices with their start and end apart: 3, of which 3 were waited for; matrix products, arithmetic and copies ran while one was open for 0% of the time, Pallas kernels for 0%

profile of v1, /device:TPU:163, one launch (start us, length us, event | category | flops | bytes accessed | tf_op | source)
XLA Modules:
  0.0 1145.0 jit_solution(1361647887658678445)
XLA Ops:
  7.3 1.4 copy.85
  10.0 35.2 %custom-call.17 = f32[3,128,128]{2,1,0:T(8,128)S(1)} custom-call(f32[3,128,128]{2,1,0:T(8,128)S(1)} %cholesky.122), custom_call_target="Cholesky" | custom-call | tf_op jit(solution)/shard_map/jit(cholesky)/cholesky | solution.py:17
  45.2 29.5 %custom-call.18 = f32[3,1,128,128]{2,3,1,0:T(8,128)S(1)} custom-call(f32[3,1,128,128]{3,2,1,0:T(8,128)S(1)} %select_bitcast_fusion), custom_call_target="InvertDiagBlocksLowerTriangular" | custom-call | tf_op jit(solution)/shard_map/jit(cholesky)/cholesky | solution.py:17
  75.6 35.2 %custom-call.19 = f32[3,128,128]{2,1,0:T(8,128)S(1)} custom-call(f32[3,128,128]{2,1,0:T(8,128)S(1)} %convolution_subtract_fusion), custom_call_target="Cholesky" | custom-call | tf_op jit(solution)/shard_map/jit(cholesky)/cholesky | solution.py:17
  112.1 45.2 %all-gather.2.cloned.1.call-done = f32[24,256,256]{2,1,0:T(8,128)} async-done(((f32[3,256,256]{2,1,0:T(8,128)}), f32[24,256,256]{2,1,0:T(8,128)}) %all-gather.2.cloned.1.call-update) | async-done | bytes 6291472 | tf_op jit(solution)/shard_map/all_gather | solution.py:18
  157.3 6.3 broadcast_select_fusion
  163.7 10.5 while.1
  164.3 5.0 bitcast_dynamic-update-slice_fusion.2
  169.8 4.4 bitcast_dynamic-update-slice_fusion.2
  174.2 473.0 %custom-call.20 = f32[24,2,128,128]{2,3,1,0:T(8,128)} custom-call(f32[24,2,128,128]{3,2,1,0:T(8,128)} %bitcast.95), custom_call_target="InvertDiagBlocksLowerTriangular" | custom-call | tf_op jit(solution)/shard_map/jit(_solve_triangular)/vmap()/triangular_solve | solution.py:19
  647.2 2.9 fusion.32
  650.2 4.9 fusion.8
  655.1 1.5 fusion.11
  658.0 4.8 stack.2
  662.8 5.4 all-to-all-start
  670.2 103.0 %all-to-all-done = bf16[8,24,96,256]{3,2,1,0:T(8,128)(2,1)} async-done(((bf16[8,24,96,256]{3,2,1,0:T(8,128)(2,1)}), bf16[8,24,96,256]{3,2,1,0:T(8,128)(2,1)}, u32[]{:S(2)}, u32[]{:S(2)}) %all-to-all-start) | async-done | bytes 9437216 | tf_op jit(solution)/shard_map/all_to_all | solution.py:49
  773.2 8.6 copy.94
  781.8 11.8 %fusion = bf16[24,1,128,256]{3,1,2,0:T(2,128)(2,1)} fusion(pred[24,6,1,1]{1,2,3,0:T(4,128)(4,1)S(1)} %copy.102, bf16[24,6,128,256]{3,2,1,0:T(8,128)(2,1)} %bitcast.87), kind=kOutput, calls=%fused_computation.3 | convolution fusion | flops 9437184 | bytes 11010192 | tf_op jit(solution)/shard_map/...tp,...pbw->...tbw/dot_general | solution.py:55
  793.6 6.1 convolution_convert_fusion
  799.7 9.5 gather_fusion
  809.2 11.0 select_select_fusion
  820.2 9.2 all-to-all-start.1
  830.6 293.8 %all-to-all-done.1 = bf16[32,2,768,128]{3,2,1,0:T(8,128)(2,1)} async-done(((bf16[32,2,768,128]{3,2,1,0:T(8,128)(2,1)}), bf16[32,2,768,128]{3,2,1,0:T(8,128)(2,1)}, u32[]{:S(2)}, u32[]{:S(2)}) %all-to-all-start.1) | async-done | bytes 12582944 | tf_op jit(solution)/shard_map/all_to_all | solution.py:67
  1124.3 12.8 %fusion.12 = f32[8,128,128]{2,0,1:T(8,128)S(1)} fusion(bf16[32,2,6,128,128]{4,3,2,1,0:T(8,128)(2,1)} %bitcast.26, s32[32,2,6]{0,2,1:T(8,128)S(1)} %select_reduce_fusion.2, pred[32,2]{0,1:T(4,128)(4,1)S(1)} %get-tuple-element.21), kind=kOutput, calls=%fused_computation.19 | convolution fusion | flops 100669440 | bytes 13108800 | tf_op jit(solution)/shard_map/smfp,smpic->fic/dot_general | solution.py:73
  (60 shorter events, 10.2 us)
Async XLA Ops:
  7.2 150.1 %all-gather.2.cloned.1.call-start = ((), (), s32[]{:S(2)}) async-start(), calls=%async_computation.2 | async-start | bytes 7077888 | tf_op jit(solution)/shard_map/all_gather | solution.py:18
  163.7 483.6 %copy-start.2 = (f32[1,24,96,256]{3,2,1,0:T(8,128)S(1)}, f32[1,24,96,256]{3,2,1,0:T(8,128)}, u32[]{:S(2)}) copy-start(f32[1,24,96,256]{3,2,1,0:T(8,128)} %param.6) | copy-start | bytes 7077892
  650.1 5.0 copy-start.1
  662.8 5.4 copy-start.5
  662.8 7.1 copy-start.4
  662.8 110.4 %all-to-all-start = ((bf16[8,24,96,256]{3,2,1,0:T(8,128)(2,1)}), bf16[8,24,96,256]{3,2,1,0:T(8,128)(2,1)}, u32[]{:S(2)}, u32[]{:S(2)}) async-start(bf16[8,24,96,256]{3,2,1,0:T(8,128)(2,1)} %stack.2), calls=%async_computation | async-start | bytes 18874368 | tf_op jit(solution)/shard_map/all_to_all | solution.py:49
  781.8 11.8 %copy-start = (bf16[8,24,96,256]{3,2,0,1:T(8,128)(2,1)S(1)}, bf16[8,24,96,256]{3,2,0,1:T(8,128)(2,1)}, u32[]{:S(2)}) copy-start(bf16[8,24,96,256]{3,2,0,1:T(8,128)(2,1)} %copy.94) | copy-start | bytes 28311556
  820.2 304.1 %all-to-all-start.1 = ((bf16[32,2,768,128]{3,2,1,0:T(8,128)(2,1)}), bf16[32,2,768,128]{3,2,1,0:T(8,128)(2,1)}, u32[]{:S(2)}, u32[]{:S(2)}) async-start(bf16[32,2,768,128]{3,2,1,0:T(8,128)(2,1)} %select_select_fusion), calls=%async_computation.1 | async-start | bytes 25165824 | tf_op jit(solution)/shard_map/all_to_all | solution.py:67
  1124.3 12.9 %copy-start.3 = (f32[1,1024,128]{2,1,0:T(8,128)S(1)}, f32[1,1024,128]{2,1,0:T(8,128)}, u32[]{:S(2)}) copy-start(f32[1,1024,128]{2,1,0:T(8,128)} %param.9) | copy-start | bytes 1572868
Sparse Core Ops, SparseCore 0:
  112.2 45.0 all-gather.1
